TPU v7x, 32 devices: a whole 2x2x4 slice. The times are simulated.
32 devices in a mesh: ctx: 8 (over y, x, core), exp: 4 (over z).
Axes of the slice: x: 2, y: 2, z: 4, core: 2. Of those that a mesh axis runs over, the one named last changes fastest.
Arguments:
- queries: bfloat16 [1024, 6144], P('ctx', 'exp'), may hold values from -0.71875 to 0.71875
- keys: bfloat16 [1024, 6144], P('ctx', 'exp'), may hold values from -0.71875 to 0.71875
- values: bfloat16 [1024, 6144], P('ctx', 'exp'), may hold values from -0.71875 to 0.71875
- out_grad: bfloat16 [1024, 6144], P('ctx', 'exp'), may hold values from -0.71875 to 0.71875
- log_decay: float32 [1024, 48], P('ctx', 'exp'), may hold values from -1.6 to 0, as said below
- moe_grad: bfloat16 [1024, 6144], P('ctx', 'exp'), may hold values from -6 to 6
- expert_ids: int32 [1024, 2], P('ctx'), may hold values from 0 to 3, all different within a row; in each aligned block of 128 rows (0 to 127, 128 to 255, ...) at most 80 rows name the same one
- gate_weights: float32 [1024, 2], P('ctx'), may hold values from 0.2 to 1
- down_weight: bfloat16 [8, 3072, 6144], P('ctx', 'exp'), may hold values from -0.078125 to 0.078125
Outputs:
- query_grad: bfloat16 [1024, 6144], P('ctx', 'exp')
- key_grad: bfloat16 [1024, 6144], P('ctx', 'exp')
- value_grad: bfloat16 [1024, 6144], P('ctx', 'exp')
- hidden_grad: bfloat16 [8, 640, 3072], P('ctx', None, 'exp')
Inputs may be any that keep to these rules, and one draw needn't show every extreme that they name: `expert_ids`: in the rows of one device (aligned blocks of 128 tokens) no expert is named more than 80 times, and in every draw some expert is named exactly 80 times in some block; a token's two experts differ. `log_decay`: every entry is negative.
All inputs are finite; a program needn't handle non-finite values.
Results may differ from a plain program's by a relative error of at most 0.0049.
Values may be sent and summed in bfloat16 or wider, within the bound.
A program may use at most 128 MiB of HBM per device.

v0:
```python
import jax
import jax.numpy as jnp
from jax import lax
from jax.sharding import PartitionSpec as P


def carried_in(x, axis, combine, identity, reverse):
    devices, place = (lax.axis_size(axis), lax.axis_index(axis))
    everything = jax.tree.map(lambda part: lax.all_gather(part, axis), x)
    start = jax.tree.map(
        lambda part, zero: jnp.broadcast_to(jnp.asarray(zero, part.dtype), part.shape), x, identity
    )

    def turn(k, before):
        at = devices - 1 - k if reverse else k
        reached = at > place if reverse else at < place
        new = combine(before, jax.tree.map(lambda part: part[at], everything))
        return jax.tree.map(lambda a, b: jnp.where(reached, a, b), new, before)

    return lax.fori_loop(0, devices, turn, start)


def partner_2(value, axis, apart):
    mask = 2**apart
    pairs = [(source, source ^ mask) for source in range(lax.axis_size(axis))]
    return lax.ppermute(value, axis, pairs)


def combine_states(earlier, later):
    return (later[1][:, None, None] * earlier[0] + later[0], earlier[1] * later[1])


def attention_grads(queries, keys, values, out_grad, log_decay):
    length, head_count = log_decay.shape
    head_size = queries.shape[1] // head_count
    query_h = queries.reshape(length, head_count, head_size)
    key_h = keys.reshape(length, head_count, head_size)
    value_h = values.reshape(length, head_count, head_size)
    grad_h = out_grad.reshape(length, head_count, head_size)
    running = jnp.cumsum(log_decay, axis=0)
    closing = running[-1]
    causal = jnp.arange(length)[:, None] >= jnp.arange(length)[None, :]
    spread = running.T[:, :, None] - running.T[:, None, :]
    weights = jnp.where(causal[None], jnp.exp(jnp.where(causal[None], spread, 0.0)), 0.0)
    until_finish = jnp.exp(closing[None, :] - running)
    since_beginning = jnp.exp(running)
    query_full = query_h.astype(jnp.float32)
    key_full = key_h.astype(jnp.float32)
    value_full = value_h.astype(jnp.float32)
    gradient_full = grad_h.astype(jnp.float32)
    block_state = jnp.einsum(
        "jqz,jqb->qzb",
        key_full * until_finish[:, :, None],
        value_full,
        precision=lax.Precision.HIGHEST,
    )
    block_grad = jnp.einsum(
        "soj,sop->ojp",
        query_full * since_beginning[:, :, None],
        gradient_full,
        precision=lax.Precision.HIGHEST,
    )
    block_decay = jnp.exp(closing)
    identity_pair = (jnp.zeros_like(block_state), jnp.ones_like(block_decay))
    leading_part, _ = carried_in(
        (block_state, block_decay), "ctx", combine_states, identity_pair, False
    )
    trailing_part, _ = carried_in(
        (block_grad, block_decay), "ctx", combine_states, identity_pair, True
    )
    grad_scores = (
        jnp.einsum("thv,shv->hts", grad_h, value_h, preferred_element_type=jnp.float32) * weights
    ).astype(jnp.bfloat16)
    scores = (
        jnp.einsum("thk,shk->hts", query_h, key_h, preferred_element_type=jnp.float32) * weights
    ).astype(jnp.bfloat16)
    query_grad = jnp.einsum(
        "hts,shk->thk", grad_scores, key_h, preferred_element_type=jnp.float32
    ) + since_beginning[:, :, None] * jnp.einsum(
        "xrq,rgq->xrg", gradient_full, leading_part, precision=lax.Precision.HIGHEST
    )
    key_grad = jnp.einsum(
        "hts,thk->shk", grad_scores, query_h, preferred_element_type=jnp.float32
    ) + until_finish[:, :, None] * jnp.einsum(
        "pox,ofx->pof", value_full, trailing_part, precision=lax.Precision.HIGHEST
    )
    value_grad = jnp.einsum(
        "hts,thv->shv", scores, grad_h, preferred_element_type=jnp.float32
    ) + until_finish[:, :, None] * jnp.einsum(
        "raj,ajb->rab", key_full, trailing_part, precision=lax.Precision.HIGHEST
    )
    flat_width = head_count * head_size
    return (
        query_grad.reshape(length, flat_width).astype(jnp.bfloat16),
        key_grad.reshape(length, flat_width).astype(jnp.bfloat16),
        value_grad.reshape(length, flat_width).astype(jnp.bfloat16),
    )


def route_rows(moe_grad, expert_ids, gate_weights, experts, capacity):
    pair_ids = expert_ids.reshape(-1)
    onehot = (pair_ids[:, None] == jnp.arange(experts)[None, :]).astype(jnp.int32)
    earlier = jnp.cumsum(onehot, axis=0) - onehot
    pair_slots = (pair_ids * capacity + jnp.sum(earlier * onehot, axis=1)).reshape(-1, 2)
    slot_iota = jnp.arange(experts * capacity)[:, None]
    first_table = jnp.where(
        slot_iota == pair_slots[:, 0][None, :], gate_weights[:, 0][None, :], 0.0
    )
    second_table = jnp.where(
        slot_iota == pair_slots[:, 1][None, :], gate_weights[:, 1][None, :], 0.0
    )
    dispatch_table = first_table + second_table
    return jnp.dot(
        dispatch_table, moe_grad.astype(jnp.float32), precision=lax.Precision.HIGHEST
    ).astype(jnp.bfloat16)


def per_device(
    queries, keys, values, out_grad, log_decay, moe_grad, expert_ids, gate_weights, down_weight
):
    query_grad, key_grad, value_grad = attention_grads(queries, keys, values, out_grad, log_decay)
    devices_ctx = lax.axis_size("ctx")
    experts = devices_ctx // 2
    length = moe_grad.shape[0]
    capacity = 5 * length // (2 * experts)
    routed = route_rows(moe_grad, expert_ids, gate_weights, experts, capacity)
    weight_slab = down_weight[0]
    half_count = capacity // 2
    own_rows = lax.all_to_all(routed, "ctx", split_axis=0, concat_axis=0, tiled=True)
    own_full = lax.all_gather(own_rows, "exp", axis=1, tiled=True)
    partner = partner_2(own_full, "ctx", 0)
    parity = lax.axis_index("ctx") % 2
    own_view = own_full.reshape(devices_ctx, half_count, -1)
    partner_view = partner.reshape(devices_ctx, half_count, -1)
    lower_half = jnp.where(parity == 0, own_view, partner_view)
    upper_half = jnp.where(parity == 0, partner_view, own_view)
    all_rows = jnp.concatenate([lower_half, upper_half], axis=1).reshape(devices_ctx * capacity, -1)
    hidden = jnp.einsum("sd,fd->sf", all_rows, weight_slab, preferred_element_type=jnp.float32)
    hidden_grad = hidden.astype(jnp.bfloat16)[None]
    return (query_grad, key_grad, value_grad, hidden_grad)


def solution(mesh):
    in_specs = (
        P("ctx", "exp"),
        P("ctx", "exp"),
        P("ctx", "exp"),
        P("ctx", "exp"),
        P("ctx", "exp"),
        P("ctx", "exp"),
        P("ctx", None),
        P("ctx", None),
        P("ctx", "exp", None),
    )
    out_specs = (P("ctx", "exp"), P("ctx", "exp"), P("ctx", "exp"), P("ctx", None, "exp"))
    return jax.shard_map(
        per_device, mesh=mesh, in_specs=in_specs, out_specs=out_specs, check_vma=False
    )
```

profile of v0, /device:TPU:0, one launch (start us, length us, event | category | flops | bytes accessed | tf_op | source)
XLA Modules:
  0.0 227.5 jit_solution(2332480826886481344)
XLA Ops:
  12.7 19.7 %all_to_all.12 = bf16[8,40,1536]{2,1,0:T(8,128)(2,1)} all-to-all(bf16[8,40,1536]{2,1,0:T(8,128)(2,1)S(1)} %bitcast.133), channel_id=1, replica_groups=mesh['ctx'=8,'exp'=4] {'ctx'}, dimensions={0} | all-to-all | bytes 1966080 | tf_op jit(solution)/shard_map/all_to_all | solution.py:129
  36.5 1.9 fusion.21
  38.5 69.9 %all-gather.7.cloned.1.call-done = bf16[320,6144]{1,0:T(8,128)(2,1)} async-done(((bf16[320,1536]{1,0:T(8,128)(2,1)}), bf16[320,6144]{1,0:T(8,128)(2,1)}) %all-gather.7.cloned.1.call-update) | async-done | bytes 3932176 | tf_op jit(solution)/shard_map/all_gather | solution.py:130
  108.9 1.8 fusion.24
  110.8 1.5 copy.121
  112.3 10.4 %all-gather.2 = f32[8,1,12]{2,1,0:T(1,128)} all-gather(f32[1,1,12]{2,1,0:T(1,128)} %get-tuple-element.313), channel_id=1, replica_groups=mesh['ctx'=8,'exp'=4] {'ctx'}, dimensions={0}, use_global_device_ids=true | all-gather | bytes 432 | tf_op jit(solution)/shard_map/all_gather | solution.py:9
  123.4 2.0 fusion.19
  125.4 5.6 %broadcast_select_fusion.1 = (bf16[320,6144]{1,0:T(8,128)(2,1)}, bf16[320,6144]{1,0:T(8,128)(2,1)}) fusion(bf16[320,6144]{1,0:T(8,128)(2,1)} %all-gather.7.cloned.1.call-done, bf16[320,6144]{1,0:T(8,128)(2,1)} %collective-permute-done, pred[]{:T(512)S(6)} %eq.61), kind=kLoop, calls=%fused_computation.10 | loop fusion | flops 3932160 | bytes 15728641 | tf_op jit(solution)/shard_map/jit(_where)/select_n | solution.py:135
  130.9 7.8 %pad_maximum_fusion = bf16[8,80,6144]{2,1,0:T(8,128)(2,1)} fusion(bf16[8,40,6144]{2,1,0:T(8,128)(2,1)} %bitcast.126, bf16[8,40,6144]{2,1,0:T(8,128)(2,1)} %bitcast.125), kind=kLoop, calls=%fused_computation.8 | loop fusion | flops 15728640 | bytes 15728640 | tf_op jit(solution)/shard_map/concatenate | solution.py:137
  138.7 12.3 %fusion.7 = bf16[1,640,768]{2,1,0:T(8,128)(2,1)} fusion(bf16[640,6144]{1,0:T(8,128)(2,1)} %bitcast.127, bf16[1,768,6144]{2,1,0:T(8,128)(2,1)} %param.21), kind=kOutput, calls=%fused_computation.13 | convolution fusion | flops 6040289280 | bytes 18284544 | tf_op jit(solution)/shard_map/sd,fd->sf/dot_general | solution.py:138
  150.9 3.5 %all-gather.11.cloned.1.call-done = f32[96,128,128]{2,1,0:T(8,128)} async-done(((f32[12,128,128]{2,1,0:T(8,128)}), f32[96,128,128]{2,1,0:T(8,128)}) %all-gather.11.cloned.1.call-update) | async-done | bytes 6291472 | tf_op jit(solution)/shard_map/all_gather | solution.py:9
  154.4 20.2 %while.31 = (s32[]{:T(128)}, f32[12,128,128]{2,1,0:T(8,128)S(1)}, s32[]{:T(128)}, f32[8,12]{1,0:T(8,128)}, f32[8,12,128,128]{3,2,1,0:T(8,128)}, /*index=5*/s32[]{:T(128)}, s32[]{:T(128)}, s32[]{:T(128)}, s32[]{:T(128)}) while((s32[]{:T(128)}, f32[12,128,128]{2,1,0:T(8,128)S(1)}, s32[]{:T(128)}, f32[8,12]{1,0:T(8,128)}, ...), condition=%wide.region_4.5_spmd.clone, body=%wide.region_3.4_spmd.clone.sunk | while | flops 786440 | bytes 2359607 | solution.py:20
  155.6 1.3 fusion.69
  158.1 1.3 fusion.69
  160.6 1.3 fusion.69
  163.1 1.4 fusion.69
  165.7 1.3 fusion.69
  168.3 1.3 fusion.69
  170.8 1.3 fusion.69
  173.3 1.3 fusion.69
  174.6 1.7 fusion.15
  176.3 2.5 %fusion.18 = bf16[128,12,128]{0,2,1:T(8,128)(2,1)} fusion(f32[128,12,128]{0,2,1:T(8,128)} %fusion.15, bf16[128,12,128]{0,2,1:T(8,128)(2,1)S(1)} %bitcast.139, bf16[128,12,128]{0,2,1:T(8,128)(2,1)S(1)} %bitcast.135, bf16[128,12,128]{0,2,1:T(8,128)(2,1)S(1)} %bitcast.130, f32[12,128]{1,0:T(8,128)} %copy.121, pred[128,128]{1,0:T(8,128)(4,1)} %copy-done.6), kind=kOutput, calls=%fused_computation.30 | convolution fusion | flops 102039552 | bytes 2381824 | tf_op jit(solution)/shard_map/hts,thv->shv/dot_general | solution.py:87
  178.8 1.9 copy.142
  180.7 1.4 fusion.14
  182.1 19.8 %all-gather.9.cloned.1.call-done = f32[96,128,128]{2,1,0:T(8,128)} async-done(((f32[12,128,128]{2,1,0:T(8,128)}), f32[96,128,128]{2,1,0:T(8,128)}) %all-gather.9.cloned.1.call-update) | async-done | bytes 6291472 | tf_op jit(solution)/shard_map/all_gather | solution.py:9
  201.9 16.1 %while.30 = (s32[]{:T(128)}, f32[12,128,128]{2,1,0:T(8,128)S(1)}, s32[]{:T(128)}, f32[8,12]{1,0:T(8,128)}, f32[8,12,128,128]{3,2,1,0:T(8,128)}, /*index=5*/s32[]{:T(128)}, s32[]{:T(128)}) while((s32[]{:T(128)}, f32[12,128,128]{2,1,0:T(8,128)S(1)}, s32[]{:T(128)}, f32[8,12]{1,0:T(8,128)}, f32[8,12,128,128]{3,2,1,0:T(8,128)}, ...), condition=%wide.region_2.3_spmd.clone, body=%wide.region_1.2_spmd.clone.sunk | while | flops 786436 | bytes 2359545 | solution.py:20
  202.6 1.3 fusion.68
  204.6 1.3 fusion.68
  206.7 1.3 fusion.68
  208.7 1.3 fusion.68
  210.7 1.3 fusion.68
  212.7 1.3 fusion.68
  (76 shorter events, 31.5 us)
Async XLA Ops:
  7.2 4.6 %copy-start = (bf16[128,1536]{1,0:T(8,128)(2,1)S(1)}, bf16[128,1536]{1,0:T(8,128)(2,1)}, u32[]{:S(2)}) copy-start(bf16[128,1536]{1,0:T(8,128)(2,1)} %param.18) | copy-start | bytes 1179652
  7.2 101.3 %copy-start.4 = (bf16[128,1536]{1,0:T(8,128)(2,1)S(1)}, bf16[128,1536]{1,0:T(8,128)(2,1)}, u32[]{:S(2)}) copy-start(bf16[128,1536]{1,0:T(8,128)(2,1)} %param.14) | copy-start | bytes 1179652
  7.2 101.5 %copy-start.5 = (bf16[128,1536]{1,0:T(8,128)(2,1)S(1)}, bf16[128,1536]{1,0:T(8,128)(2,1)}, u32[]{:S(2)}) copy-start(bf16[128,1536]{1,0:T(8,128)(2,1)} %param.15) | copy-start | bytes 1179652
  7.2 101.2 %all-gather.7.cloned.1.call-start = ((), (), s32[]{:S(2)}) async-start(), calls=%async_computation.1 | async-start | bytes 4915200 | tf_op jit(solution)/shard_map/all_gather | solution.py:130
  32.4 122.0 %all-gather.11.cloned.1.call-start = ((), (), s32[]{:S(2)}) async-start(), calls=%async_computation.3 | async-start | bytes 7077888 | tf_op jit(solution)/shard_map/all_gather | solution.py:9
  33.4 74.9 %copy-start.3 = (f32[128,12]{1,0:T(8,128)}, f32[128,12]{1,0:T(8,128)S(1)}, u32[]{:S(2)}) copy-start(f32[128,12]{1,0:T(8,128)S(1)} %reduce_window_sum.26) | copy-start | bytes 18436
  38.4 163.4 %all-gather.9.cloned.1.call-start = ((), (), s32[]{:S(2)}) async-start(), calls=%async_computation.2 | async-start | bytes 7077888 | tf_op jit(solution)/shard_map/all_gather | solution.py:9
  108.4 17.0 %collective-permute-start = (bf16[320,6144]{1,0:T(8,128)(2,1)}, bf16[320,6144]{1,0:T(8,128)(2,1)}, u32[]{:S(2)}, u32[]{:S(2)}) collective-permute-start(bf16[320,6144]{1,0:T(8,128)(2,1)} %all-gather.7.cloned.1.call-done), channel_id=1, source_target_pairs={{0,4},{4,0},{8,12},{12,8},{16,20},{20,16},{24,28},{28,24},{1,5},{5... | collective-permute-start | bytes 11796488 | tf_op jit(solution)/shard_map/ppermute | solution.py:26
  122.8 0.6 copy-start.6
  201.9 16.6 %copy-start.2 = (bf16[12,128,128]{2,1,0:T(8,128)(2,1)S(1)}, bf16[12,128,128]{2,1,0:T(8,128)(2,1)}, u32[]{:S(2)}) copy-start(bf16[12,128,128]{2,1,0:T(8,128)(2,1)} %fusion.19) | copy-start | bytes 1179652
  201.9 18.0 %copy-start.1 = (f32[128,12,128]{0,2,1:T(8,128)S(1)}, f32[128,12,128]{0,2,1:T(8,128)}, u32[]{:S(2)}) copy-start(f32[128,12,128]{0,2,1:T(8,128)} %fusion.14) | copy-start | bytes 2359300
Sparse Core Ops, SparseCore 0:
  32.5 75.7 all-gather.6
  110.3 44.0 all-gather.10
  156.3 45.5 all-gather.8
where the time goes:
time: 229 us; the launch traced here: 228 us
  waiting for transfers between devices  93.2 us (41%)
  other arithmetic  36.5 us (16%)
  blocking collectives  30.2 us (13%)
  local copies, waits for them, and re-layouts  27.8 us (12%)
  matrix products  25.5 us (11%)
  between operations  14 us (6%)
    all_gather x1, waiting for transfers between devices, per_device(): own_full = lax.all_gather(own_rows, 'exp', axis=1, tiled=True)  69.9 us
    all_gather x2, waiting for transfers between devices, carried_in(): everything = jax.tree.map(lambda part: lax.all_gather(part, axis), x)  23.2 us
    select_n x16, other arithmetic, turn(): return jax.tree.map(lambda a, b: jnp.where(reached, a, b), new, before)  20.9 us
    all_to_all x1, blocking collectives, per_device(): lax.all_to_all(routed, 'ctx', split_axis=0, concat_axis=0, tiled=True)  19.7 us
    mul x16, local copies, waits for them, and re-layouts, combine_states(): later[1][:, None, None] * earlier[0] + later[0]  15.1 us
    dot_general x1, matrix products, per_device(): jnp.einsum('sd,fd->sf', all_rows, weight_slab, preferred_element_type=jnp...  12.3 us
    all_gather x1, blocking collectives, carried_in(): everything = jax.tree.map(lambda part: lax.all_gather(part, axis), x)  10.4 us
    unnamed x23, local copies, waits for them, and re-layouts  8.98 us
  transfers between devices with their start and end apart: 4, of which 3 were waited for; matrix products, arithmetic and copies ran while one was open for 28% of the time, Pallas kernels for 0%

commit v1 on v0

--- a/solution.py
+++ b/solution.py
@@ -1,6 +1,10 @@
+import functools
+
 import jax
 import jax.numpy as jnp
 from jax import lax
+from jax.experimental import pallas as pl
+from jax.experimental.pallas import tpu as pltpu
 from jax.sharding import PartitionSpec as P
 
 
@@ -140,6 +144,569 @@
     return (query_grad, key_grad, value_grad, hidden_grad)
 
 
+MESH = pl.DeviceIdType.MESH
+NT = (((1,), (1,)), ((), ()))
+NN = (((1,), (0,)), ((), ()))
+TN = (((0,), (0,)), ((), ()))
+
+
+def mm(a, b, dims, precision=None):
+    return lax.dot_general(a, b, dims, precision=precision, preferred_element_type=jnp.float32)
+
+
+def split_bf16(x):
+    high = x.astype(jnp.bfloat16)
+    return high, (x - high.astype(jnp.float32)).astype(jnp.bfloat16)
+
+
+def causal_mask(size):
+    return lax.broadcasted_iota(jnp.int32, (size, size), 0) >= lax.broadcasted_iota(
+        jnp.int32, (size, size), 1
+    )
+
+
+def fused_kernel(
+    sizes,
+    q_ref,
+    k_ref,
+    v_ref,
+    g_ref,
+    ld_ref,
+    moe_ref,
+    ids_ref,
+    gate_ref,
+    w_hbm,
+    qg_ref,
+    kg_ref,
+    vg_ref,
+    hid_ref,
+    wbuf,
+    raw,
+    sendbuf,
+    rows,
+    acc,
+    table,
+    slot_gate,
+    run_col,
+    run_row,
+    close_row,
+    own_decay,
+    sib_decay,
+    chip_decay,
+    far_decay,
+    state,
+    sib_state,
+    chip_state,
+    far_state,
+    pair_state,
+    y_state,
+    outer,
+    local,
+    w_sem,
+    own_send,
+    fwd_send,
+    raw_recv,
+    xy_send,
+    xy_recv,
+    sib_send,
+    sib_recv,
+    lvl_send,
+    lvl_recv,
+):
+    n_z, n_chip, cap, heads, size = sizes
+    half = heads // 2
+    length = moe_ref.shape[0]
+    width = moe_ref.shape[1]
+    c, z = lax.axis_index("ctx"), lax.axis_index("exp")
+    core = c % 2
+    chip = c // 2
+    xbit, ybit = chip % 2, chip // 2
+    sib = c + 1 - 2 * core
+    xpart = c + 2 - 4 * xbit
+    ypart = c + 4 - 8 * ybit
+    has_left, has_right = z > 0, z < n_z - 1
+
+    def chip_at(d):
+        return (chip + d) % n_chip
+
+    barrier = pltpu.get_barrier_semaphore()
+    for d in range(1, n_chip):
+        pl.semaphore_signal(
+            barrier, inc=1, device_id={"ctx": chip_at(d) * 2 + core}, device_id_type=MESH
+        )
+    pl.semaphore_signal(barrier, inc=1, device_id={"ctx": sib}, device_id_type=MESH)
+
+    @pl.when(has_left)
+    def _():
+        pl.semaphore_signal(barrier, inc=1, device_id={"exp": z - 1}, device_id_type=MESH)
+
+    @pl.when(has_right)
+    def _():
+        pl.semaphore_signal(barrier, inc=1, device_id={"exp": z + 1}, device_id_type=MESH)
+
+    line_peers = jnp.minimum(z, 1) + jnp.minimum(n_z - 1 - z, 1)
+    pl.semaphore_wait(barrier, n_chip + line_peers)
+
+    def own_copy(side):
+        return pltpu.make_async_remote_copy(
+            src_ref=moe_ref,
+            dst_ref=raw.at[z],
+            send_sem=own_send.at[side],
+            recv_sem=raw_recv.at[z],
+            device_id={"exp": z - 1 + 2 * side},
+            device_id_type=MESH,
+        )
+
+    @pl.when(has_left)
+    def _():
+        own_copy(0).start()
+
+    @pl.when(has_right)
+    def _():
+        own_copy(1).start()
+
+    w_copies = [
+        pltpu.make_async_copy(w_hbm.at[0, :, pl.ds(i * width, width)], wbuf.at[i], w_sem.at[i])
+        for i in range(n_z)
+    ]
+    for copy in w_copies:
+        copy.start()
+
+    mirrored = jnp.where(2 * z < n_z, z, n_z - 1 - z)
+
+    def chunk_at(i):
+        if i == 0:
+            return z
+        near = mirrored + (i + 1) // 2 if i % 2 else mirrored - i // 2
+        from_low = jnp.where(i <= 2 * mirrored, near, i)
+        return jnp.where(2 * z < n_z, from_low, n_z - 1 - from_low)
+
+    ids = ids_ref[...]
+    gates = gate_ref[...]
+    expert = lax.broadcasted_iota(jnp.int32, (length, 128), 1)
+    first, second = ids[:, 0:1] == expert, ids[:, 1:2] == expert
+    named = (first | second).astype(jnp.float32)
+    weight = jnp.where(first, gates[:, 0:1], 0.0) + jnp.where(second, gates[:, 1:2], 0.0)
+    t_row = lax.broadcasted_iota(jnp.int32, (length, length), 0)
+    t_col = lax.broadcasted_iota(jnp.int32, (length, length), 1)
+    earlier = (t_row < t_col).astype(jnp.float32)
+    rank_row = mm(named, earlier, TN)
+    named_row = named.T
+    weight_row = weight.T
+    slot = lax.broadcasted_iota(jnp.int32, (cap, length), 0).astype(jnp.float32)
+    for e in range(n_chip):
+        hit = (rank_row[e : e + 1, :] == slot) & (named_row[e : e + 1, :] > 0.5)
+        table[e] = hit.astype(jnp.float32).astype(jnp.bfloat16)
+        gate = jnp.sum(jnp.where(hit, weight_row[e : e + 1, :], 0.0), axis=1, keepdims=True)
+        slot_gate[e] = jnp.broadcast_to(gate, (cap, 128))
+
+    def xy_copy(i, s, d):
+        return pltpu.make_async_remote_copy(
+            src_ref=sendbuf.at[i, d - 1],
+            dst_ref=rows.at[s, c],
+            send_sem=xy_send.at[i, d],
+            recv_sem=xy_recv.at[s, chip],
+            device_id={"ctx": chip_at(d) * 2 + core},
+            device_id_type=MESH,
+        )
+
+    def xy_arrival(i, s, d):
+        source = chip_at(d)
+        return pltpu.make_async_remote_copy(
+            src_ref=sendbuf.at[i, d - 1],
+            dst_ref=rows.at[s, source * 2 + core],
+            send_sem=xy_send.at[i, d],
+            recv_sem=xy_recv.at[s, source],
+            device_id={"ctx": source * 2 + core},
+            device_id_type=MESH,
+        )
+
+    def sib_copy(s, d):
+        block = rows.at[s, chip_at(d) * 2 + core]
+        return pltpu.make_async_remote_copy(
+            src_ref=block,
+            dst_ref=block,
+            send_sem=sib_send.at[s, d],
+            recv_sem=sib_recv.at[s, d],
+            device_id={"ctx": sib},
+            device_id_type=MESH,
+        )
+
+    def sib_arrival(s, d):
+        block = rows.at[s, chip_at(d) * 2 + 1 - core]
+        return pltpu.make_async_remote_copy(
+            src_ref=block,
+            dst_ref=block,
+            send_sem=sib_send.at[s, d],
+            recv_sem=sib_recv.at[s, d],
+            device_id={"ctx": sib},
+            device_id_type=MESH,
+        )
+
+    def forward_copy(i, s, side):
+        return pltpu.make_async_remote_copy(
+            src_ref=raw.at[s],
+            dst_ref=raw.at[s],
+            send_sem=fwd_send.at[i],
+            recv_sem=raw_recv.at[s],
+            device_id={"exp": z - 1 + 2 * side},
+            device_id_type=MESH,
+        )
+
+    def forwards(s):
+        return (s < z) & has_right, (s > z) & has_left
+
+    def route_chunk(i):
+        s = chunk_at(i)
+        if i:
+            pltpu.make_async_remote_copy(
+                src_ref=raw.at[s],
+                dst_ref=raw.at[s],
+                send_sem=fwd_send.at[i],
+                recv_sem=raw_recv.at[s],
+                device_id={"exp": s},
+                device_id_type=MESH,
+            ).wait_recv()
+            to_right, to_left = forwards(s)
+
+            @pl.when(to_right)
+            def _():
+                forward_copy(i, s, 1).start()
+
+            @pl.when(to_left)
+            def _():
+                forward_copy(i, s, 0).start()
+
+        for d in (*range(1, n_chip), 0):
+            e = chip_at(d)
+            picked = mm(table[e], raw[s] if i else moe_ref[...], NN)
+            routed = (picked * slot_gate[e][:, 0:1]).astype(jnp.bfloat16)
+            if d:
+                sendbuf[i, d - 1] = routed
+                xy_copy(i, s, d).start()
+            else:
+                rows[s, c] = routed
+                sib_copy(s, 0).start()
+
+    def pass_on(i):
+        s = chunk_at(i)
+        for d in range(1, n_chip):
+            xy_arrival(i, s, d).wait_recv()
+            sib_copy(s, d).start()
+
+    def multiply(i):
+        s = chunk_at(i)
+        for d in range(n_chip):
+            sib_arrival(s, d).wait_recv()
+        if i == 0:
+            for copy in w_copies:
+                copy.wait()
+
+        def tile(j, carry):
+            left = rows[s, pl.ds(2 * j, 2)].reshape(2 * cap, width)
+            part = mm(left, wbuf[s], NT)
+            if i:
+                part = part + acc[j]
+            if i < n_z - 1:
+                acc[j] = part
+            else:
+                hid_ref[0, pl.ds(pl.multiple_of(j * 2 * cap, 2 * cap), 2 * cap), :] = part.astype(
+                    jnp.bfloat16
+                )
+            return carry
+
+        lax.fori_loop(0, n_chip, tile, 0)
+
+    route_chunk(0)
+
+    log_decay = ld_ref[...]
+    highest = lax.Precision.HIGHEST
+    lower = (t_row >= t_col).astype(jnp.float32)
+    upper = (t_row <= t_col).astype(jnp.float32)
+    running = mm(lower, log_decay, NN, highest)
+    running_t = mm(log_decay, upper, TN, highest)
+    closing = mm(log_decay, jnp.ones((length, size), jnp.float32), TN, highest)
+    for h in range(heads):
+        run_col[h] = jnp.broadcast_to(running[:, h : h + 1], (length, size))
+        run_row[h] = jnp.broadcast_to(running_t[h : h + 1, :], (8, length))
+        close_row[h] = jnp.broadcast_to(closing[h : h + 1, :], (8, size))
+        own_decay[h] = jnp.broadcast_to(jnp.exp(closing[h : h + 1, :]), (8, size))
+
+    group = 4 if heads % 4 == 0 else 2
+
+    def per_head(body):
+        def turn(i, carry):
+            for u in range(group):
+                h = i * group + u
+                body(h, pl.ds(pl.multiple_of(h * size, size), size))
+            return carry
+
+        lax.fori_loop(0, heads // group, turn, 0)
+
+    def block_states(h, cols):
+        along = run_col[h]
+        until = jnp.exp(close_row[h][0:1, :] - along)
+        since = jnp.exp(along)
+        key_high, key_low = split_bf16(k_ref[:, cols].astype(jnp.float32) * until)
+        query_high, query_low = split_bf16(q_ref[:, cols].astype(jnp.float32) * since)
+        value, grad = v_ref[:, cols], g_ref[:, cols]
+        state[0, h] = mm(key_high, value, TN) + mm(key_low, value, TN)
+        state[1, h] = mm(query_high, grad, TN) + mm(query_low, grad, TN)
+
+    per_head(block_states)
+
+    def level(index, src, dst, peer):
+        return pltpu.make_async_remote_copy(
+            src_ref=src,
+            dst_ref=dst,
+            send_sem=lvl_send.at[index],
+            recv_sem=lvl_recv.at[index],
+            device_id={"ctx": peer},
+            device_id_type=MESH,
+        )
+
+    core_state = level(0, state, sib_state, sib)
+    core_decay = level(1, own_decay, sib_decay, sib)
+    x_state = level(2, chip_state, far_state, xpart)
+    x_decay = level(3, chip_decay, far_decay, xpart)
+    y_copy = level(4, pair_state.at[ybit], y_state, ypart)
+    outer_copy = level(5, outer.at[core], outer.at[core], sib)
+    outer_arrival = level(5, outer.at[1 - core], outer.at[1 - core], sib)
+    core_state.start()
+    core_decay.start()
+
+    def local_parts(h, cols):
+        mask = causal_mask(length)
+        spread = run_col[h] - run_row[h][0:1, :]
+        weights = jnp.where(mask, jnp.exp(jnp.where(mask, spread, 0.0)), 0.0)
+        query, key, value, grad = q_ref[:, cols], k_ref[:, cols], v_ref[:, cols], g_ref[:, cols]
+        grad_scores = (mm(grad, value, NT) * weights).astype(jnp.bfloat16)
+        scores = (mm(query, key, NT) * weights).astype(jnp.bfloat16)
+        local[0, :, cols] = mm(grad_scores, key, NN)
+        local[1, :, cols] = mm(grad_scores, query, TN)
+        local[2, :, cols] = mm(scores, grad, TN)
+
+    core_state.wait_recv()
+    core_decay.wait_recv()
+    chip_decay[...] = own_decay[...] * sib_decay[...]
+
+    def chip_totals(j, carry):
+        h = core * half + j
+        mine, theirs = own_decay[h][0:1, :], sib_decay[h][0:1, :]
+        s_mine, s_sib = state[0, h], sib_state[0, h]
+        g_mine, g_sib = state[1, h], sib_state[1, h]
+        first_core = core == 0
+        chip_state[0, j] = jnp.where(
+            first_core, s_sib + theirs * s_mine, s_mine + mine * s_sib
+        ).astype(jnp.bfloat16)
+        chip_state[1, j] = jnp.where(
+            first_core, g_mine + mine * g_sib, g_sib + theirs * g_mine
+        ).astype(jnp.bfloat16)
+        return carry
+
+    lax.fori_loop(0, half, chip_totals, 0)
+    x_state.start()
+    x_decay.start()
+
+    if n_z > 1:
+        route_chunk(1)
+    per_head(local_parts)
+
+    x_state.wait_recv()
+    x_decay.wait_recv()
+
+    def pair_totals(j, carry):
+        h = core * half + j
+        mine, theirs = chip_decay[h][0:1, :], far_decay[h][0:1, :]
+        s_mine, s_far = chip_state[0, j].astype(jnp.float32), far_state[0, j].astype(jnp.float32)
+        g_mine, g_far = chip_state[1, j].astype(jnp.float32), far_state[1, j].astype(jnp.float32)
+        first_x = xbit == 0
+        pair_state[0, j] = jnp.where(
+            first_x, s_far + theirs * s_mine, s_mine + mine * s_far
+        ).astype(jnp.bfloat16)
+        pair_state[1, j] = jnp.where(
+            first_x, g_mine + mine * g_far, g_far + theirs * g_mine
+        ).astype(jnp.bfloat16)
+        return carry
+
+    lax.fori_loop(0, half, pair_totals, 0)
+    y_copy.start()
+
+    pass_on(0)
+    if n_z > 2:
+        route_chunk(2)
+    multiply(0)
+
+    y_copy.wait_recv()
+
+    def outer_states(j, carry):
+        h = core * half + j
+        theirs = far_decay[h][0:1, :]
+        from_y = y_state[j].astype(jnp.float32)
+        zero = jnp.zeros_like(from_y)
+        y_prefix = jnp.where(ybit == 1, from_y, zero)
+        y_suffix = jnp.where(ybit == 0, from_y, zero)
+        s_far, g_far = far_state[0, j].astype(jnp.float32), far_state[1, j].astype(jnp.float32)
+        outer[core, 0, j] = jnp.where(xbit == 1, s_far + theirs * y_prefix, y_prefix)
+        outer[core, 1, j] = jnp.where(xbit == 0, g_far + theirs * y_suffix, y_suffix)
+        return carry
+
+    lax.fori_loop(0, half, outer_states, 0)
+    outer_copy.start()
+
+    if n_z > 1:
+        pass_on(1)
+    for i in range(3, n_z):
+        route_chunk(i)
+        multiply(i - 2)
+        pass_on(i - 1)
+
+    outer_arrival.wait_recv()
+
+    def finish(h, cols):
+        along = run_col[h]
+        until = jnp.exp(close_row[h][0:1, :] - along)
+        since = jnp.exp(along)
+        theirs = sib_decay[h][0:1, :]
+        side, j = h // half, h % half
+        before, after = outer[side, 0, j], outer[side, 1, j]
+        prefix = jnp.where(core == 1, sib_state[0, h] + theirs * before, before)
+        suffix = jnp.where(core == 0, sib_state[1, h] + theirs * after, after)
+        prefix_high, prefix_low = split_bf16(prefix)
+        suffix_high, suffix_low = split_bf16(suffix)
+        key, value, grad = k_ref[:, cols], v_ref[:, cols], g_ref[:, cols]
+        query_part = mm(grad, prefix_high, NT) + mm(grad, prefix_low, NT)
+        key_part = mm(value, suffix_high, NT) + mm(value, suffix_low, NT)
+        value_part = mm(key, suffix_high, NN) + mm(key, suffix_low, NN)
+        qg_ref[:, cols] = (local[0, :, cols] + since * query_part).astype(jnp.bfloat16)
+        kg_ref[:, cols] = (local[1, :, cols] + until * key_part).astype(jnp.bfloat16)
+        vg_ref[:, cols] = (local[2, :, cols] + until * value_part).astype(jnp.bfloat16)
+
+    per_head(finish)
+    if n_z > 2:
+        multiply(n_z - 2)
+        pass_on(n_z - 1)
+    multiply(n_z - 1)
+
+    @pl.when(has_left)
+    def _():
+        own_copy(0).wait_send()
+
+    @pl.when(has_right)
+    def _():
+        own_copy(1).wait_send()
+
+    for i in range(n_z):
+        s = chunk_at(i)
+        if i:
+            to_right, to_left = forwards(s)
+
+            @pl.when(to_right)
+            def _():
+                forward_copy(i, s, 1).wait_send()
+
+            @pl.when(to_left)
+            def _():
+                forward_copy(i, s, 0).wait_send()
+
+        for d in range(1, n_chip):
+            xy_copy(i, s, d).wait_send()
+        for d in range(n_chip):
+            sib_copy(s, d).wait_send()
+    for copy in (core_state, core_decay, x_state, x_decay, y_copy, outer_copy):
+        copy.wait_send()
+
+
+def fused(
+    queries, keys, values, out_grad, log_decay, moe_grad, expert_ids, gate_weights, down_weight
+):
+    n_ctx, n_z = lax.axis_size("ctx"), lax.axis_size("exp")
+    n_chip = n_ctx // 2
+    length, heads = log_decay.shape
+    width = moe_grad.shape[1]
+    size = queries.shape[1] // heads
+    cap = 5 * length // (2 * n_chip)
+    half = heads // 2
+    hidden = down_weight.shape[1]
+    bf16, f32 = jnp.bfloat16, jnp.float32
+    dma = pltpu.SemaphoreType.DMA
+    vmem = pl.BlockSpec(memory_space=pltpu.VMEM)
+    decay = pltpu.VMEM((heads, 8, size), f32)
+    scratch = [
+        pltpu.VMEM((n_z, hidden, width), bf16),
+        pltpu.VMEM((n_z, length, width), bf16),
+        pltpu.VMEM((n_z, n_chip - 1, cap, width), bf16),
+        pltpu.VMEM((n_z, n_ctx, cap, width), bf16),
+        pltpu.VMEM((n_chip, 2 * cap, hidden), f32),
+        pltpu.VMEM((n_chip, cap, length), bf16),
+        pltpu.VMEM((n_chip, cap, 128), f32),
+        pltpu.VMEM((heads, length, size), f32),
+        pltpu.VMEM((heads, 8, length), f32),
+        decay,
+        decay,
+        decay,
+        decay,
+        decay,
+        pltpu.VMEM((2, heads, size, size), f32),
+        pltpu.VMEM((2, heads, size, size), f32),
+        pltpu.VMEM((2, half, size, size), bf16),
+        pltpu.VMEM((2, half, size, size), bf16),
+        pltpu.VMEM((2, half, size, size), bf16),
+        pltpu.VMEM((half, size, size), bf16),
+        pltpu.VMEM((2, 2, half, size, size), f32),
+        pltpu.VMEM((3, length, width), f32),
+        dma((n_z,)),
+        dma((2,)),
+        dma((n_z,)),
+        dma((n_z,)),
+        dma((n_z, n_chip)),
+        dma((n_z, n_chip)),
+        dma((n_z, n_chip)),
+        dma((n_z, n_chip)),
+        dma((6,)),
+        dma((6,)),
+    ]
+    flat = jax.ShapeDtypeStruct((length, heads * size), bf16)
+    return pl.pallas_call(
+        functools.partial(fused_kernel, (n_z, n_chip, cap, heads, size)),
+        out_shape=(
+            flat,
+            flat,
+            flat,
+            jax.ShapeDtypeStruct((1, n_ctx * cap, hidden), bf16),
+        ),
+        in_specs=[vmem] * 8 + [pl.BlockSpec(memory_space=pl.ANY)],
+        out_specs=(vmem,) * 4,
+        scratch_shapes=scratch,
+        compiler_params=pltpu.CompilerParams(
+            collective_id=0, has_side_effects=True, vmem_limit_bytes=52 * 2**20
+        ),
+    )(queries, keys, values, out_grad, log_decay, moe_grad, expert_ids, gate_weights, down_weight)
+
+
+def body(
+    queries, keys, values, out_grad, log_decay, moe_grad, expert_ids, gate_weights, down_weight
+):
+    n_ctx, n_z = lax.axis_size("ctx"), lax.axis_size("exp")
+    length, heads = log_decay.shape
+    cap = 5 * length // n_ctx
+    args = (
+        queries, keys, values, out_grad, log_decay, moe_grad, expert_ids, gate_weights, down_weight
+    )
+    size = queries.shape[1] // heads
+    fits = (
+        n_ctx == 8
+        and n_z > 2
+        and cap % 16 == 0
+        and size == 128
+        and length == 128
+        and heads % 2 == 0
+        and moe_grad.shape[1] % 128 == 0
+        and queries.shape[1] == moe_grad.shape[1]
+    )
+    return fused(*args) if fits else per_device(*args)
+
+
 def solution(mesh):
     in_specs = (
         P("ctx", "exp"),
@@ -154,5 +721,5 @@
     )
     out_specs = (P("ctx", "exp"), P("ctx", "exp"), P("ctx", "exp"), P("ctx", None, "exp"))
     return jax.shard_map(
-        per_device, mesh=mesh, in_specs=in_specs, out_specs=out_specs, check_vma=False
-    )
+        body, mesh=mesh, in_specs=in_specs, out_specs=out_specs, check_vma=False
+    )

time: 229 us -> 74.6 us (0.33)
  waiting for transfers between devices: 93.2 us -> 0 us
  Pallas kernels: 0 us -> 65.6 us
  other arithmetic: 36.5 us -> 0 us
  blocking collectives: 30.2 us -> 0 us
  matrix products: 25.5 us -> 0 us
  local copies, waits for them, and re-layouts: 27.8 us -> 7.81 us
  between operations: 14 us -> 0.65 us
    all_gather x3 -> x0, waiting for transfers between devices: 93.1 us -> none  [the longest x1 69.9 us: per_device(): own_full = lax.all_gather(own_rows, 'exp', axis=1, tiled=True)]
    pallas_call x0 -> x1, Pallas kernels: none -> 65.6 us  [fused(): pl.pallas_call(functools.partial(fused_kernel, (n_z, n_chip, cap, heads,...]
    select_n x17 -> x0, other arithmetic: 26.4 us -> none  [the longest x16 20.9 us: turn(): return jax.tree.map(lambda a, b: jnp.where(reached, a, b), new, before)]
    dot_general x11 -> x0, matrix products: 25.5 us -> none  [the longest x1 12.3 us: per_device(): jnp.einsum('sd,fd->sf', all_rows, weight_slab, preferred_element_type=jnp...]
    all_to_all x1 -> x0, blocking collectives: 19.7 us -> none  [per_device(): lax.all_to_all(routed, 'ctx', split_axis=0, concat_axis=0, tiled=True)]
    mul x16 -> x0, local copies, waits for them, and re-layouts: 15.1 us -> none  [combine_states(): later[1][:, None, None] * earlier[0] + later[0]]
    all_gather x1 -> x0, blocking collectives: 10.4 us -> none  [carried_in(): everything = jax.tree.map(lambda part: lax.all_gather(part, axis), x)]
    concatenate x1 -> x0, other arithmetic: 7.75 us -> none  [per_device(): jnp.concatenate([lower_half, upper_half], axis=1)]
  transfers between devices with their start and end apart: 4 -> 0, of which waited for: 3 -> 0; matrix products, arithmetic and copies ran while one was open for 28% -> 0% of each run, Pallas kernels for 0% -> 0%
where the time goes in v1:
time: 74.6 us; the launch traced here: 74 us
  Pallas kernels  65.6 us (88%)
  local copies, waits for them, and re-layouts  7.81 us (10%)
    pallas_call x1, Pallas kernels, fused(): pl.pallas_call(functools.partial(fused_kernel, (n_z, n_chip, cap, heads,...  65.6 us
    unnamed x9, local copies, waits for them, and re-layouts  7.81 us

profile of v1, /device:TPU:0, one launch (start us, length us, event | category | flops | bytes accessed | tf_op | source)
XLA Modules:
  0.0 74.0 jit_solution(14176751057203919661)
XLA Ops:
  0.6 0.8 %copy.13.ld_ref = f32[128,12]{1,0:T(8,128)S(1)} copy(f32[128,12]{0,1:T(8,128)} %param.13) | data formatting | bytes 12288 | tf_op args[4]
  1.4 0.8 %copy.14.ids_ref = s32[128,2]{1,0:T(8,128)S(1)} copy(s32[128,2]{0,1:T(2,128)} %param.15) | data formatting | bytes 2048 | tf_op args[6]
  2.2 0.8 %copy.15.gate_ref = f32[128,2]{1,0:T(8,128)S(1)} copy(f32[128,2]{0,1:T(2,128)} %param.16) | data formatting | bytes 2048 | tf_op args[7]
  3.0 0.0 copy-start
  3.0 1.0 %copy-done = bf16[128,1536]{1,0:T(8,128)(2,1)S(1)} copy-done((bf16[128,1536]{1,0:T(8,128)(2,1)S(1)}, bf16[128,1536]{1,0:T(8,128)(2,1)}, u32[]{:S(2)}) %copy-start) | copy-done | bytes 393240
  4.0 65.6 %shard_map.120 = (bf16[128,1536]{1,0:T(8,128)(2,1)S(1)}, bf16[128,1536]{1,0:T(8,128)(2,1)S(1)}, bf16[128,1536]{1,0:T(8,128)(2,1)S(1)}, bf16[1,640,768]{2,1,0:T(8,128)(2,1)}) custom-call(bf16[128,1536]{1,0:T(8,128)(2,1)S(1)} %copy-done, bf16[128,1536]{1,0:T(8,128)(2,1)} %k_ref.1, bf16[128,1536]{1,0:T(8,128)(2,1)} %v_ref.1, bf16[128,1536]{1,0:T(8,128)(2,1)} %g_ref.1, ...), custom_call_target="tpu_custom_call" | custom-call | tf_op jit(solution)/shard_map/pallas_call | solution.py:670
  69.6 0.7 %copy.20 = bf16[128,1536]{1,0:T(8,128)(2,1)} copy(bf16[128,1536]{1,0:T(8,128)(2,1)S(1)} %get-tuple-element.8) | data formatting | bytes 786432
  70.3 0.7 %copy.21 = bf16[128,1536]{1,0:T(8,128)(2,1)} copy(bf16[128,1536]{1,0:T(8,128)(2,1)S(1)} %get-tuple-element.9) | data formatting | bytes 786432
  71.1 0.7 %copy.22 = bf16[128,1536]{1,0:T(8,128)(2,1)} copy(bf16[128,1536]{1,0:T(8,128)(2,1)S(1)} %get-tuple-element.10) | data formatting | bytes 786432
  71.8 2.2 %copy.23 = bf16[1,640,768]{2,1,0:T(8,128)(2,1)} copy(bf16[1,640,768]{2,1,0:T(8,128)(2,1)} %get-tuple-element.11) | data formatting | bytes 1966080
Async XLA Ops:
  3.0 1.0 %copy-start = (bf16[128,1536]{1,0:T(8,128)(2,1)S(1)}, bf16[128,1536]{1,0:T(8,128)(2,1)}, u32[]{:S(2)}) copy-start(bf16[128,1536]{1,0:T(8,128)(2,1)} %q_ref.1) | copy-start | bytes 1179652

commit v2 on v1

--- a/solution.py
+++ b/solution.py
@@ -204,10 +204,13 @@
     local,
     w_sem,
     own_send,
+    relay_send,
     fwd_send,
     raw_recv,
     xy_send,
     xy_recv,
+    zp_send,
+    zp_recv,
     sib_send,
     sib_recv,
     lvl_send,
@@ -224,7 +227,11 @@
     sib = c + 1 - 2 * core
     xpart = c + 2 - 4 * xbit
     ypart = c + 4 - 8 * ybit
-    has_left, has_right = z > 0, z < n_z - 1
+    upper_half, odd = z // 2, z % 2
+    partner = z + 1 - 2 * odd
+    across = n_z - 1 - z
+    inner = odd + upper_half - 2 * odd * upper_half
+    toward = z + 1 - 2 * upper_half
 
     def chip_at(d):
         return (chip + d) % n_chip
@@ -236,34 +243,27 @@
         )
     pl.semaphore_signal(barrier, inc=1, device_id={"ctx": sib}, device_id_type=MESH)
 
-    @pl.when(has_left)
+    pl.semaphore_signal(barrier, inc=1, device_id={"exp": partner}, device_id_type=MESH)
+
+    @pl.when(inner == 1)
     def _():
-        pl.semaphore_signal(barrier, inc=1, device_id={"exp": z - 1}, device_id_type=MESH)
-
-    @pl.when(has_right)
-    def _():
-        pl.semaphore_signal(barrier, inc=1, device_id={"exp": z + 1}, device_id_type=MESH)
-
-    line_peers = jnp.minimum(z, 1) + jnp.minimum(n_z - 1 - z, 1)
-    pl.semaphore_wait(barrier, n_chip + line_peers)
-
-    def own_copy(side):
+        pl.semaphore_signal(barrier, inc=1, device_id={"exp": across}, device_id_type=MESH)
+
+    pl.semaphore_wait(barrier, n_chip + 1 + inner)
+
+    def raw_copy(src, s, send_sem, to):
         return pltpu.make_async_remote_copy(
-            src_ref=moe_ref,
-            dst_ref=raw.at[z],
-            send_sem=own_send.at[side],
-            recv_sem=raw_recv.at[z],
-            device_id={"exp": z - 1 + 2 * side},
+            src_ref=src,
+            dst_ref=raw.at[s],
+            send_sem=send_sem,
+            recv_sem=raw_recv.at[s],
+            device_id={"exp": to},
             device_id_type=MESH,
         )
 
-    @pl.when(has_left)
-    def _():
-        own_copy(0).start()
-
-    @pl.when(has_right)
-    def _():
-        own_copy(1).start()
+    own_copy = raw_copy(moe_ref, z, own_send, toward)
+    own_copy.start()
+    relay_copy = raw_copy(raw.at[partner], partner, relay_send, across)
 
     w_copies = [
         pltpu.make_async_copy(w_hbm.at[0, :, pl.ds(i * width, width)], wbuf.at[i], w_sem.at[i])
@@ -272,27 +272,23 @@
     for copy in w_copies:
         copy.start()
 
-    mirrored = jnp.where(2 * z < n_z, z, n_z - 1 - z)
-
     def chunk_at(i):
-        if i == 0:
-            return z
-        near = mirrored + (i + 1) // 2 if i % 2 else mirrored - i // 2
-        from_low = jnp.where(i <= 2 * mirrored, near, i)
-        return jnp.where(2 * z < n_z, from_low, n_z - 1 - from_low)
+        return 1 + i + upper_half * (1 - 2 * i) if i else z
+
+    def forward_copy(i):
+        s = chunk_at(i)
+        return raw_copy(raw.at[s], s, fwd_send.at[i], partner)
 
     ids = ids_ref[...]
     gates = gate_ref[...]
-    expert = lax.broadcasted_iota(jnp.int32, (length, 128), 1)
-    first, second = ids[:, 0:1] == expert, ids[:, 1:2] == expert
-    named = (first | second).astype(jnp.float32)
-    weight = jnp.where(first, gates[:, 0:1], 0.0) + jnp.where(second, gates[:, 1:2], 0.0)
+    expert = lax.broadcasted_iota(jnp.int32, (8, length), 0)
+    first, second = ids[0:1, :] == expert, ids[1:2, :] == expert
+    named_row = (first | second).astype(jnp.float32)
+    weight_row = jnp.where(first, gates[0:1, :], 0.0) + jnp.where(second, gates[1:2, :], 0.0)
     t_row = lax.broadcasted_iota(jnp.int32, (length, length), 0)
     t_col = lax.broadcasted_iota(jnp.int32, (length, length), 1)
     earlier = (t_row < t_col).astype(jnp.float32)
-    rank_row = mm(named, earlier, TN)
-    named_row = named.T
-    weight_row = weight.T
+    rank_row = mm(named_row, earlier, NN)
     slot = lax.broadcasted_iota(jnp.int32, (cap, length), 0).astype(jnp.float32)
     for e in range(n_chip):
         hit = (rank_row[e : e + 1, :] == slot) & (named_row[e : e + 1, :] > 0.5)
@@ -343,40 +339,26 @@
             device_id_type=MESH,
         )
 
-    def forward_copy(i, s, side):
+    def zp_copy(s, d):
+        block = rows.at[s, chip_at(d) * 2 + core]
         return pltpu.make_async_remote_copy(
-            src_ref=raw.at[s],
-            dst_ref=raw.at[s],
-            send_sem=fwd_send.at[i],
-            recv_sem=raw_recv.at[s],
-            device_id={"exp": z - 1 + 2 * side},
+            src_ref=block,
+            dst_ref=block,
+            send_sem=zp_send.at[d],
+            recv_sem=zp_recv.at[d],
+            device_id={"exp": partner},
             device_id_type=MESH,
         )
 
-    def forwards(s):
-        return (s < z) & has_right, (s > z) & has_left
+    def take(i):
+        forward_copy(i).wait_recv()
+
+        @pl.when(inner == 1)
+        def _():
+            forward_copy(i).start()
 
     def route_chunk(i):
         s = chunk_at(i)
-        if i:
-            pltpu.make_async_remote_copy(
-                src_ref=raw.at[s],
-                dst_ref=raw.at[s],
-                send_sem=fwd_send.at[i],
-                recv_sem=raw_recv.at[s],
-                device_id={"exp": s},
-                device_id_type=MESH,
-            ).wait_recv()
-            to_right, to_left = forwards(s)
-
-            @pl.when(to_right)
-            def _():
-                forward_copy(i, s, 1).start()
-
-            @pl.when(to_left)
-            def _():
-                forward_copy(i, s, 0).start()
-
         for d in (*range(1, n_chip), 0):
             e = chip_at(d)
             picked = mm(table[e], raw[s] if i else moe_ref[...], NN)
@@ -394,28 +376,26 @@
             xy_arrival(i, s, d).wait_recv()
             sib_copy(s, d).start()
 
-    def multiply(i):
-        s = chunk_at(i)
-        for d in range(n_chip):
-            sib_arrival(s, d).wait_recv()
-        if i == 0:
+    def multiply(s, first=False, last=False):
+        if first:
             for copy in w_copies:
                 copy.wait()
 
-        def tile(j, carry):
+        def tile(j):
             left = rows[s, pl.ds(2 * j, 2)].reshape(2 * cap, width)
             part = mm(left, wbuf[s], NT)
-            if i:
+            if not first:
                 part = part + acc[j]
-            if i < n_z - 1:
-                acc[j] = part
-            else:
+            if last:
                 hid_ref[0, pl.ds(pl.multiple_of(j * 2 * cap, 2 * cap), 2 * cap), :] = part.astype(
                     jnp.bfloat16
                 )
-            return carry
-
-        lax.fori_loop(0, n_chip, tile, 0)
+            else:
+                acc[j] = part
+
+        for d in range(n_chip):
+            sib_arrival(s, d).wait_recv()
+            tile(chip_at(d))
 
     route_chunk(0)
 
@@ -423,9 +403,9 @@
     highest = lax.Precision.HIGHEST
     lower = (t_row >= t_col).astype(jnp.float32)
     upper = (t_row <= t_col).astype(jnp.float32)
-    running = mm(lower, log_decay, NN, highest)
-    running_t = mm(log_decay, upper, TN, highest)
-    closing = mm(log_decay, jnp.ones((length, size), jnp.float32), TN, highest)
+    running = mm(lower, log_decay, NT, highest)
+    running_t = mm(log_decay, upper, NN, highest)
+    closing = mm(log_decay, jnp.ones((length, size), jnp.float32), NN, highest)
     for h in range(heads):
         run_col[h] = jnp.broadcast_to(running[:, h : h + 1], (length, size))
         run_row[h] = jnp.broadcast_to(running_t[h : h + 1, :], (8, length))
@@ -485,6 +465,13 @@
         local[0, :, cols] = mm(grad_scores, key, NN)
         local[1, :, cols] = mm(grad_scores, query, TN)
         local[2, :, cols] = mm(scores, grad, TN)
+
+    @pl.when(inner == 1)
+    def _():
+        relay_copy.wait_recv()
+        relay_copy.start()
+
+    take(1)
 
     core_state.wait_recv()
     core_decay.wait_recv()
@@ -508,9 +495,13 @@
     x_state.start()
     x_decay.start()
 
-    if n_z > 1:
-        route_chunk(1)
+    route_chunk(1)
+    pass_on(0)
     per_head(local_parts)
+    take(2)
+    for d in range(n_chip):
+        zp_copy(z, d).start()
+    multiply(z, first=True)
 
     x_state.wait_recv()
     x_decay.wait_recv()
@@ -532,10 +523,7 @@
     lax.fori_loop(0, half, pair_totals, 0)
     y_copy.start()
 
-    pass_on(0)
-    if n_z > 2:
-        route_chunk(2)
-    multiply(0)
+    route_chunk(2)
 
     y_copy.wait_recv()
 
@@ -554,12 +542,8 @@
     lax.fori_loop(0, half, outer_states, 0)
     outer_copy.start()
 
-    if n_z > 1:
-        pass_on(1)
-    for i in range(3, n_z):
-        route_chunk(i)
-        multiply(i - 2)
-        pass_on(i - 1)
+    pass_on(1)
+    multiply(chunk_at(1))
 
     outer_arrival.wait_recv()
 
@@ -583,36 +567,30 @@
         vg_ref[:, cols] = (local[2, :, cols] + until * value_part).astype(jnp.bfloat16)
 
     per_head(finish)
-    if n_z > 2:
-        multiply(n_z - 2)
-        pass_on(n_z - 1)
-    multiply(n_z - 1)
-
-    @pl.when(has_left)
+    pass_on(2)
+    multiply(chunk_at(2))
+    for d in range(n_chip):
+        zp_copy(partner, d).wait_recv()
+        sib_copy(partner, d).start()
+    multiply(partner, last=True)
+
+    own_copy.wait_send()
+
+    @pl.when(inner == 1)
     def _():
-        own_copy(0).wait_send()
-
-    @pl.when(has_right)
-    def _():
-        own_copy(1).wait_send()
-
-    for i in range(n_z):
+        relay_copy.wait_send()
+        for i in range(1, n_z - 1):
+            forward_copy(i).wait_send()
+
+    for i in range(n_z - 1):
         s = chunk_at(i)
-        if i:
-            to_right, to_left = forwards(s)
-
-            @pl.when(to_right)
-            def _():
-                forward_copy(i, s, 1).wait_send()
-
-            @pl.when(to_left)
-            def _():
-                forward_copy(i, s, 0).wait_send()
-
         for d in range(1, n_chip):
             xy_copy(i, s, d).wait_send()
         for d in range(n_chip):
             sib_copy(s, d).wait_send()
+    for d in range(n_chip):
+        zp_copy(z, d).wait_send()
+        sib_copy(partner, d).wait_send()
     for copy in (core_state, core_decay, x_state, x_decay, y_copy, outer_copy):
         copy.wait_send()
 
@@ -635,7 +613,7 @@
     scratch = [
         pltpu.VMEM((n_z, hidden, width), bf16),
         pltpu.VMEM((n_z, length, width), bf16),
-        pltpu.VMEM((n_z, n_chip - 1, cap, width), bf16),
+        pltpu.VMEM((n_z - 1, n_chip - 1, cap, width), bf16),
         pltpu.VMEM((n_z, n_ctx, cap, width), bf16),
         pltpu.VMEM((n_chip, 2 * cap, hidden), f32),
         pltpu.VMEM((n_chip, cap, length), bf16),
@@ -656,11 +634,14 @@
         pltpu.VMEM((2, 2, half, size, size), f32),
         pltpu.VMEM((3, length, width), f32),
         dma((n_z,)),
-        dma((2,)),
+        dma,
+        dma,
+        dma((n_z - 1,)),
         dma((n_z,)),
-        dma((n_z,)),
+        dma((n_z - 1, n_chip)),
         dma((n_z, n_chip)),
-        dma((n_z, n_chip)),
+        dma((n_chip,)),
+        dma((n_chip,)),
         dma((n_z, n_chip)),
         dma((n_z, n_chip)),
         dma((6,)),
@@ -681,7 +662,17 @@
         compiler_params=pltpu.CompilerParams(
             collective_id=0, has_side_effects=True, vmem_limit_bytes=52 * 2**20
         ),
-    )(queries, keys, values, out_grad, log_decay, moe_grad, expert_ids, gate_weights, down_weight)
+    )(
+        queries,
+        keys,
+        values,
+        out_grad,
+        log_decay.T,
+        moe_grad,
+        expert_ids.T,
+        gate_weights.T,
+        down_weight,
+    )
 
 
 def body(
@@ -696,7 +687,7 @@
     size = queries.shape[1] // heads
     fits = (
         n_ctx == 8
-        and n_z > 2
+        and n_z == 4
         and cap % 16 == 0
         and size == 128
         and length == 128

time: 74.6 us -> 81.2 us (1.088)
  Pallas kernels: 65.6 us -> 71.7 us
    pallas_call x1, Pallas kernels: 65.6 us -> 71.7 us  [fused(): pl.pallas_call(functools.partial(fused_kernel, (n_z, n_chip, cap, heads,...]
    unnamed x9 -> x14, local copies, waits for them, and re-layouts: 7.81 us -> 8.48 us
where the time goes in v2:
time: 81.2 us; the launch traced here: 80.9 us
  Pallas kernels  71.7 us (88%)
  local copies, waits for them, and re-layouts  8.48 us (10%)
    pallas_call x1, Pallas kernels, fused(): pl.pallas_call(functools.partial(fused_kernel, (n_z, n_chip, cap, heads,...  71.7 us
    unnamed x14, local copies, waits for them, and re-layouts  8.48 us

profile of v2, /device:TPU:0, one launch (start us, length us, event | category | flops | bytes accessed | tf_op | source)
XLA Modules:
  0.0 80.9 jit_solution(5326127320967868277)
XLA Ops:
  0.6 0.0 copy-start
  0.6 1.0 %copy-done = bf16[128,1536]{1,0:T(8,128)(2,1)S(1)} copy-done((bf16[128,1536]{1,0:T(8,128)(2,1)S(1)}, bf16[128,1536]{1,0:T(8,128)(2,1)}, u32[]{:S(2)}) %copy-start) | copy-done | bytes 393240
  1.6 0.0 copy-start.1
  1.6 1.0 %copy-done.1 = bf16[128,1536]{1,0:T(8,128)(2,1)S(1)} copy-done((bf16[128,1536]{1,0:T(8,128)(2,1)S(1)}, bf16[128,1536]{1,0:T(8,128)(2,1)}, u32[]{:S(2)}) %copy-start.1) | copy-done | bytes 393240
  2.6 0.0 copy-start.2
  2.6 0.7 copy-done.2
  3.3 0.0 copy-start.3
  3.3 0.7 copy-done.3
  4.0 0.0 copy-start.4
  4.0 0.7 copy-done.4
  4.7 71.7 %shard_map.120 = (bf16[128,1536]{1,0:T(8,128)(2,1)S(1)}, bf16[128,1536]{1,0:T(8,128)(2,1)S(1)}, bf16[128,1536]{1,0:T(8,128)(2,1)S(1)}, bf16[1,640,768]{2,1,0:T(8,128)(2,1)}) custom-call(bf16[128,1536]{1,0:T(8,128)(2,1)S(1)} %copy-done, bf16[128,1536]{1,0:T(8,128)(2,1)S(1)} %copy-done.1, bf16[128,1536]{1,0:T(8,128)(2,1)} %v_ref.1, bf16[128,1536]{1,0:T(8,128)(2,1)} %g_ref.1, ...), custom_call_target="tpu_custom_call" | custom-call | tf_op jit(solution)/shard_map/pallas_call | solution.py:651
  76.4 0.7 copy.17
  77.2 0.7 copy.18
  77.9 0.7 copy.19
  78.7 2.2 %copy.20 = bf16[1,640,768]{2,1,0:T(8,128)(2,1)} copy(bf16[1,640,768]{2,1,0:T(8,128)(2,1)} %get-tuple-element.11) | data formatting | bytes 1966080
Async XLA Ops:
  0.6 1.0 %copy-start = (bf16[128,1536]{1,0:T(8,128)(2,1)S(1)}, bf16[128,1536]{1,0:T(8,128)(2,1)}, u32[]{:S(2)}) copy-start(bf16[128,1536]{1,0:T(8,128)(2,1)} %q_ref.1) | copy-start | bytes 1179652
  1.6 1.0 %copy-start.1 = (bf16[128,1536]{1,0:T(8,128)(2,1)S(1)}, bf16[128,1536]{1,0:T(8,128)(2,1)}, u32[]{:S(2)}) copy-start(bf16[128,1536]{1,0:T(8,128)(2,1)} %k_ref.1) | copy-start | bytes 1179652
  2.6 0.7 copy-start.2
  3.3 0.7 copy-start.3
  4.0 0.7 copy-start.4

commit v3 on v2

--- a/solution.py
+++ b/solution.py
@@ -167,25 +167,32 @@
 
 def fused_kernel(
     sizes,
-    q_ref,
-    k_ref,
-    v_ref,
-    g_ref,
+    q_hbm,
+    k_hbm,
+    v_hbm,
+    g_hbm,
     ld_ref,
     moe_ref,
     ids_ref,
     gate_ref,
     w_hbm,
-    qg_ref,
-    kg_ref,
-    vg_ref,
-    hid_ref,
+    qg_hbm,
+    kg_hbm,
+    vg_hbm,
+    hid_hbm,
+    q_ref,
+    k_ref,
+    v_ref,
+    g_ref,
+    grads,
+    hid,
     wbuf,
     raw,
     sendbuf,
     rows,
     acc,
     table,
+    near_table,
     slot_gate,
     run_col,
     run_row,
@@ -202,8 +209,13 @@
     y_state,
     outer,
     local,
+    in_sem,
+    out_sem,
+    hid_sem,
+    moe_sem,
     w_sem,
     own_send,
+    side_send,
     relay_send,
     fwd_send,
     raw_recv,
@@ -236,6 +248,17 @@
     def chip_at(d):
         return (chip + d) % n_chip
 
+    moe_copy = pltpu.make_async_copy(moe_ref, raw.at[z], moe_sem)
+    moe_copy.start()
+    in_copies = [
+        pltpu.make_async_copy(src, dst, in_sem.at[i])
+        for i, (src, dst) in enumerate(
+            ((k_hbm, k_ref), (v_hbm, v_ref), (q_hbm, q_ref), (g_hbm, g_ref))
+        )
+    ]
+    for copy in in_copies:
+        copy.start()
+
     barrier = pltpu.get_barrier_semaphore()
     for d in range(1, n_chip):
         pl.semaphore_signal(
@@ -263,6 +286,23 @@
 
     own_copy = raw_copy(moe_ref, z, own_send, toward)
     own_copy.start()
+    part = width // 2
+    low, high = pl.ds(0, part), pl.ds(part, part)
+
+    def side_copy(s):
+        return pltpu.make_async_remote_copy(
+            src_ref=moe_ref.at[:, low],
+            dst_ref=raw.at[s, :, low],
+            send_sem=side_send,
+            recv_sem=raw_recv.at[s],
+            device_id={"exp": partner},
+            device_id_type=MESH,
+        )
+
+    @pl.when(inner == 1)
+    def _():
+        side_copy(z).start()
+
     relay_copy = raw_copy(raw.at[partner], partner, relay_send, across)
 
     w_copies = [
@@ -295,11 +335,19 @@
         table[e] = hit.astype(jnp.float32).astype(jnp.bfloat16)
         gate = jnp.sum(jnp.where(hit, weight_row[e : e + 1, :], 0.0), axis=1, keepdims=True)
         slot_gate[e] = jnp.broadcast_to(gate, (cap, 128))
+    for d in range(n_chip):
+        near_table[pl.ds(d * cap, cap), :] = table[chip_at(d)]
+
+    def block_of(s, b, i):
+        return rows.at[s, b, :, low] if i == n_z - 1 else rows.at[s, b]
+
+    def sent(i, d):
+        return sendbuf.at[i, d - 1, :, low] if i == n_z - 1 else sendbuf.at[i, d - 1]
 
     def xy_copy(i, s, d):
         return pltpu.make_async_remote_copy(
-            src_ref=sendbuf.at[i, d - 1],
-            dst_ref=rows.at[s, c],
+            src_ref=sent(i, d),
+            dst_ref=block_of(s, c, i),
             send_sem=xy_send.at[i, d],
             recv_sem=xy_recv.at[s, chip],
             device_id={"ctx": chip_at(d) * 2 + core},
@@ -309,8 +357,8 @@
     def xy_arrival(i, s, d):
         source = chip_at(d)
         return pltpu.make_async_remote_copy(
-            src_ref=sendbuf.at[i, d - 1],
-            dst_ref=rows.at[s, source * 2 + core],
+            src_ref=sent(i, d),
+            dst_ref=block_of(s, source * 2 + core, i),
             send_sem=xy_send.at[i, d],
             recv_sem=xy_recv.at[s, source],
             device_id={"ctx": source * 2 + core},
@@ -340,7 +388,7 @@
         )
 
     def zp_copy(s, d):
-        block = rows.at[s, chip_at(d) * 2 + core]
+        block = rows.at[s, chip_at(d) * 2 + core, :, high]
         return pltpu.make_async_remote_copy(
             src_ref=block,
             dst_ref=block,
@@ -358,17 +406,23 @@
             forward_copy(i).start()
 
     def route_chunk(i):
-        s = chunk_at(i)
-        for d in (*range(1, n_chip), 0):
-            e = chip_at(d)
-            picked = mm(table[e], raw[s] if i else moe_ref[...], NN)
-            routed = (picked * slot_gate[e][:, 0:1]).astype(jnp.bfloat16)
-            if d:
-                sendbuf[i, d - 1] = routed
-                xy_copy(i, s, d).start()
-            else:
-                rows[s, c] = routed
-                sib_copy(s, 0).start()
+        half_only = i == n_z - 1
+        s = partner if half_only else chunk_at(i)
+        step = part // 2 if (part // 2) % 128 == 0 else part
+        for at in range(0, part if half_only else width, step):
+            cols = pl.ds(at, step)
+            picked = mm(near_table[...], raw[s, :, cols], NN)
+            for d in range(n_chip):
+                gate = slot_gate[chip_at(d)][:, 0:1]
+                routed = (picked[d * cap : (d + 1) * cap, :] * gate).astype(jnp.bfloat16)
+                if d:
+                    sendbuf[i, d - 1, :, cols] = routed
+                else:
+                    rows[s, c, :, cols] = routed
+        for d in range(1, n_chip):
+            xy_copy(i, s, d).start()
+        if not half_only:
+            sib_copy(s, 0).start()
 
     def pass_on(i):
         s = chunk_at(i)
@@ -376,6 +430,13 @@
             xy_arrival(i, s, d).wait_recv()
             sib_copy(s, d).start()
 
+    def hid_copy(j):
+        return pltpu.make_async_copy(
+            hid.at[j],
+            hid_hbm.at[0, pl.ds(pl.multiple_of(j * 2 * cap, 2 * cap), 2 * cap), :],
+            hid_sem.at[j],
+        )
+
     def multiply(s, first=False, last=False):
         if first:
             for copy in w_copies:
@@ -383,20 +444,20 @@
 
         def tile(j):
             left = rows[s, pl.ds(2 * j, 2)].reshape(2 * cap, width)
-            part = mm(left, wbuf[s], NT)
+            total = mm(left, wbuf[s], NT)
             if not first:
-                part = part + acc[j]
+                total = total + acc[j]
             if last:
-                hid_ref[0, pl.ds(pl.multiple_of(j * 2 * cap, 2 * cap), 2 * cap), :] = part.astype(
-                    jnp.bfloat16
-                )
+                hid[j] = total.astype(jnp.bfloat16)
+                hid_copy(j).start()
             else:
-                acc[j] = part
+                acc[j] = total
 
         for d in range(n_chip):
             sib_arrival(s, d).wait_recv()
             tile(chip_at(d))
 
+    moe_copy.wait()
     route_chunk(0)
 
     log_decay = ld_ref[...]
@@ -433,6 +494,8 @@
         state[0, h] = mm(key_high, value, TN) + mm(key_low, value, TN)
         state[1, h] = mm(query_high, grad, TN) + mm(query_low, grad, TN)
 
+    for copy in in_copies:
+        copy.wait()
     per_head(block_states)
 
     def level(index, src, dst, peer):
@@ -471,7 +534,11 @@
         relay_copy.wait_recv()
         relay_copy.start()
 
-    take(1)
+    @pl.when(inner == 0)
+    def _():
+        side_copy(partner).wait_recv()
+
+    route_chunk(n_z - 1)
 
     core_state.wait_recv()
     core_decay.wait_recv()
@@ -495,12 +562,19 @@
     x_state.start()
     x_decay.start()
 
+    take(1)
     route_chunk(1)
     pass_on(0)
+
+    def send_high():
+        for d in range(n_chip):
+            zp_copy(z, d).start()
+
+    pl.when(inner == 0)(send_high)
     per_head(local_parts)
     take(2)
-    for d in range(n_chip):
-        zp_copy(z, d).start()
+    pl.when(inner == 1)(send_high)
+    route_chunk(2)
     multiply(z, first=True)
 
     x_state.wait_recv()
@@ -523,7 +597,8 @@
     lax.fori_loop(0, half, pair_totals, 0)
     y_copy.start()
 
-    route_chunk(2)
+    pass_on(1)
+    multiply(chunk_at(1))
 
     y_copy.wait_recv()
 
@@ -541,9 +616,6 @@
 
     lax.fori_loop(0, half, outer_states, 0)
     outer_copy.start()
-
-    pass_on(1)
-    multiply(chunk_at(1))
 
     outer_arrival.wait_recv()
 
@@ -562,23 +634,36 @@
         query_part = mm(grad, prefix_high, NT) + mm(grad, prefix_low, NT)
         key_part = mm(value, suffix_high, NT) + mm(value, suffix_low, NT)
         value_part = mm(key, suffix_high, NN) + mm(key, suffix_low, NN)
-        qg_ref[:, cols] = (local[0, :, cols] + since * query_part).astype(jnp.bfloat16)
-        kg_ref[:, cols] = (local[1, :, cols] + until * key_part).astype(jnp.bfloat16)
-        vg_ref[:, cols] = (local[2, :, cols] + until * value_part).astype(jnp.bfloat16)
+        grads[0, :, cols] = (local[0, :, cols] + since * query_part).astype(jnp.bfloat16)
+        grads[1, :, cols] = (local[1, :, cols] + until * key_part).astype(jnp.bfloat16)
+        grads[2, :, cols] = (local[2, :, cols] + until * value_part).astype(jnp.bfloat16)
 
     per_head(finish)
+    out_copies = [
+        pltpu.make_async_copy(grads.at[i], dst, out_sem.at[i])
+        for i, dst in enumerate((qg_hbm, kg_hbm, vg_hbm))
+    ]
+    for copy in out_copies:
+        copy.start()
     pass_on(2)
     multiply(chunk_at(2))
     for d in range(n_chip):
+        if d:
+            xy_arrival(n_z - 1, partner, d).wait_recv()
         zp_copy(partner, d).wait_recv()
         sib_copy(partner, d).start()
     multiply(partner, last=True)
+    for copy in out_copies:
+        copy.wait()
+    for j in range(n_chip):
+        hid_copy(j).wait()
 
     own_copy.wait_send()
 
     @pl.when(inner == 1)
     def _():
         relay_copy.wait_send()
+        side_copy(z).wait_send()
         for i in range(1, n_z - 1):
             forward_copy(i).wait_send()
 
@@ -588,11 +673,22 @@
             xy_copy(i, s, d).wait_send()
         for d in range(n_chip):
             sib_copy(s, d).wait_send()
+    for d in range(1, n_chip):
+        xy_copy(n_z - 1, partner, d).wait_send()
     for d in range(n_chip):
         zp_copy(z, d).wait_send()
         sib_copy(partner, d).wait_send()
     for copy in (core_state, core_decay, x_state, x_decay, y_copy, outer_copy):
         copy.wait_send()
+
+
+def hand_over(*refs):
+    sems = refs[-1]
+    copies = [pltpu.make_async_copy(refs[i], refs[4 + i], sems.at[i]) for i in range(4)]
+    for copy in copies:
+        copy.start()
+    for copy in copies:
+        copy.wait()
 
 
 def fused(
@@ -609,14 +705,19 @@
     bf16, f32 = jnp.bfloat16, jnp.float32
     dma = pltpu.SemaphoreType.DMA
     vmem = pl.BlockSpec(memory_space=pltpu.VMEM)
+    hbm = pl.BlockSpec(memory_space=pl.ANY)
     decay = pltpu.VMEM((heads, 8, size), f32)
     scratch = [
+        *[pltpu.VMEM((length, heads * size), bf16)] * 4,
+        pltpu.VMEM((3, length, heads * size), bf16),
+        pltpu.VMEM((n_chip, 2 * cap, hidden), bf16),
         pltpu.VMEM((n_z, hidden, width), bf16),
         pltpu.VMEM((n_z, length, width), bf16),
-        pltpu.VMEM((n_z - 1, n_chip - 1, cap, width), bf16),
+        pltpu.VMEM((n_z, n_chip - 1, cap, width), bf16),
         pltpu.VMEM((n_z, n_ctx, cap, width), bf16),
         pltpu.VMEM((n_chip, 2 * cap, hidden), f32),
         pltpu.VMEM((n_chip, cap, length), bf16),
+        pltpu.VMEM((n_chip * cap, length), bf16),
         pltpu.VMEM((n_chip, cap, 128), f32),
         pltpu.VMEM((heads, length, size), f32),
         pltpu.VMEM((heads, 8, length), f32),
@@ -633,12 +734,17 @@
         pltpu.VMEM((half, size, size), bf16),
         pltpu.VMEM((2, 2, half, size, size), f32),
         pltpu.VMEM((3, length, width), f32),
+        dma((4,)),
+        dma((3,)),
+        dma((n_chip,)),
+        dma,
         dma((n_z,)),
+        dma,
         dma,
         dma,
         dma((n_z - 1,)),
         dma((n_z,)),
-        dma((n_z - 1, n_chip)),
+        dma((n_z, n_chip)),
         dma((n_z, n_chip)),
         dma((n_chip,)),
         dma((n_chip,)),
@@ -648,7 +754,7 @@
         dma((6,)),
     ]
     flat = jax.ShapeDtypeStruct((length, heads * size), bf16)
-    return pl.pallas_call(
+    results = pl.pallas_call(
         functools.partial(fused_kernel, (n_z, n_chip, cap, heads, size)),
         out_shape=(
             flat,
@@ -656,11 +762,11 @@
             flat,
             jax.ShapeDtypeStruct((1, n_ctx * cap, hidden), bf16),
         ),
-        in_specs=[vmem] * 8 + [pl.BlockSpec(memory_space=pl.ANY)],
-        out_specs=(vmem,) * 4,
+        in_specs=[hbm] * 4 + [vmem, hbm, vmem, vmem, hbm],
+        out_specs=(hbm,) * 4,
         scratch_shapes=scratch,
         compiler_params=pltpu.CompilerParams(
-            collective_id=0, has_side_effects=True, vmem_limit_bytes=52 * 2**20
+            collective_id=0, has_side_effects=True, vmem_limit_bytes=60 * 2**20
         ),
     )(
         queries,
@@ -673,6 +779,14 @@
         gate_weights.T,
         down_weight,
     )
+    return pl.pallas_call(
+        hand_over,
+        out_shape=tuple(jax.ShapeDtypeStruct(x.shape, x.dtype) for x in results),
+        in_specs=[hbm] * 4,
+        out_specs=(hbm,) * 4,
+        scratch_shapes=[dma((4,))],
+        compiler_params=pltpu.CompilerParams(vmem_limit_bytes=60 * 2**20),
+    )(*results)
 
 
 def body(
@@ -692,7 +806,7 @@
         and size == 128
         and length == 128
         and heads % 2 == 0
-        and moe_grad.shape[1] % 128 == 0
+        and moe_grad.shape[1] % 256 == 0
         and queries.shape[1] == moe_grad.shape[1]
     )
     return fused(*args) if fits else per_device(*args)

time: 81.2 us -> 137 us (1.69)
  Pallas kernels: 71.7 us -> 135 us
  local copies, waits for them, and re-layouts: 8.48 us -> 0 us
    pallas_call x0 -> x1, Pallas kernels: none -> 66.7 us  [fused(): pl.pallas_call(hand_over, out_shape=tuple((jax.ShapeDtypeStruct(x.shape,...]
    unnamed x14 -> x0, local copies, waits for them, and re-layouts: 8.48 us -> none
    pallas_call x1, Pallas kernels: 71.7 us -> 68.4 us  [fused(): pl.pallas_call(functools.partial(fused_kernel, (n_z, n_chip, cap, heads,...]
where the time goes in v3:
time: 137 us; the launch traced here: 136 us
  Pallas kernels  135 us (99%)
    pallas_call x1, Pallas kernels, fused(): pl.pallas_call(functools.partial(fused_kernel, (n_z, n_chip, cap, heads,...  68.4 us
    pallas_call x1, Pallas kernels, fused(): pl.pallas_call(hand_over, out_shape=tuple((jax.ShapeDtypeStruct(x.shape,...  66.7 us

profile of v3, /device:TPU:0, one launch (start us, length us, event | category | flops | bytes accessed | tf_op | source)
XLA Modules:
  0.0 135.7 jit_solution(11816929292088698683)
XLA Ops:
  0.6 68.4 %shard_map.120 = (bf16[128,1536]{1,0:T(8,128)(2,1)}, bf16[128,1536]{1,0:T(8,128)(2,1)}, bf16[128,1536]{1,0:T(8,128)(2,1)}, bf16[1,640,768]{2,1,0:T(8,128)(2,1)}) custom-call(bf16[128,1536]{1,0:T(8,128)(2,1)} %q_hbm.1, bf16[128,1536]{1,0:T(8,128)(2,1)} %k_hbm.1, bf16[128,1536]{1,0:T(8,128)(2,1)} %v_hbm.1, bf16[128,1536]{1,0:T(8,128)(2,1)} %g_hbm.1, ...), custom_call_target="tpu_custom_call" | custom-call | tf_op jit(solution)/shard_map/pallas_call | solution.py:757
  69.0 66.7 %shard_map.121 = (bf16[128,1536]{1,0:T(8,128)(2,1)}, bf16[128,1536]{1,0:T(8,128)(2,1)}, bf16[128,1536]{1,0:T(8,128)(2,1)}, bf16[1,640,768]{2,1,0:T(8,128)(2,1)}) custom-call(bf16[128,1536]{1,0:T(8,128)(2,1)} %get-tuple-element.8.refs_0_, bf16[128,1536]{1,0:T(8,128)(2,1)} %get-tuple-element.9.refs_1_, bf16[128,1536]{1,0:T(8,128)(2,1)} %get-tuple-element.10.refs_2_, ...), custom_call_target="tpu_custom_call" | custom-call | tf_op jit(solution)/shard_map/pallas_call | solution.py:782

commit v4 on v3

--- a/solution.py
+++ b/solution.py
@@ -570,10 +570,18 @@
         for d in range(n_chip):
             zp_copy(z, d).start()
 
-    pl.when(inner == 0)(send_high)
+    @pl.when(inner == 1)
+    def _():
+        forward_copy(2).wait_recv()
+        forward_copy(2).start()
+
+    send_high()
     per_head(local_parts)
-    take(2)
-    pl.when(inner == 1)(send_high)
+
+    @pl.when(inner == 0)
+    def _():
+        forward_copy(2).wait_recv()
+
     route_chunk(2)
     multiply(z, first=True)
 
@@ -683,12 +691,16 @@
 
 
 def hand_over(*refs):
-    sems = refs[-1]
-    copies = [pltpu.make_async_copy(refs[i], refs[4 + i], sems.at[i]) for i in range(4)]
-    for copy in copies:
-        copy.start()
-    for copy in copies:
-        copy.wait()
+    sources, results, stages, in_sem, out_sem = refs[:4], refs[4:8], refs[8:12], refs[12], refs[13]
+    pulls = [pltpu.make_async_copy(sources[i], stages[i], in_sem.at[i]) for i in range(4)]
+    pushes = [pltpu.make_async_copy(stages[i], results[i], out_sem.at[i]) for i in range(4)]
+    for pull in pulls:
+        pull.start()
+    for pull, push in zip(pulls, pushes):
+        pull.wait()
+        push.start()
+    for push in pushes:
+        push.wait()
 
 
 def fused(
@@ -784,7 +796,7 @@
         out_shape=tuple(jax.ShapeDtypeStruct(x.shape, x.dtype) for x in results),
         in_specs=[hbm] * 4,
         out_specs=(hbm,) * 4,
-        scratch_shapes=[dma((4,))],
+        scratch_shapes=[*[pltpu.VMEM(x.shape, x.dtype) for x in results], dma((4,)), dma((4,))],
         compiler_params=pltpu.CompilerParams(vmem_limit_bytes=60 * 2**20),
     )(*results)
 

time: 137 us -> 73 us (0.53)
  Pallas kernels: 135 us -> 70.9 us
    pallas_call x1, Pallas kernels: 66.7 us -> 2.58 us  [fused(): pl.pallas_call(hand_over, out_shape=tuple((jax.ShapeDtypeStruct(x.shape,...]
where the time goes in v4:
time: 73 us; the launch traced here: 71.6 us
  Pallas kernels  70.9 us (97%)
    pallas_call x1, Pallas kernels, fused(): pl.pallas_call(functools.partial(fused_kernel, (n_z, n_chip, cap, heads,...  68.4 us
    pallas_call x1, Pallas kernels, fused(): pl.pallas_call(hand_over, out_shape=tuple((jax.ShapeDtypeStruct(x.shape,...  2.58 us

profile of v4, /device:TPU:0, one launch (start us, length us, event | category | flops | bytes accessed | tf_op | source)
XLA Modules:
  0.0 71.6 jit_solution(15777056454066754288)
XLA Ops:
  0.6 68.4 %shard_map.120 = (bf16[128,1536]{1,0:T(8,128)(2,1)}, bf16[128,1536]{1,0:T(8,128)(2,1)}, bf16[128,1536]{1,0:T(8,128)(2,1)}, bf16[1,640,768]{2,1,0:T(8,128)(2,1)}) custom-call(bf16[128,1536]{1,0:T(8,128)(2,1)} %q_hbm.1, bf16[128,1536]{1,0:T(8,128)(2,1)} %k_hbm.1, bf16[128,1536]{1,0:T(8,128)(2,1)} %v_hbm.1, bf16[128,1536]{1,0:T(8,128)(2,1)} %g_hbm.1, ...), custom_call_target="tpu_custom_call" | custom-call | tf_op jit(solution)/shard_map/pallas_call | solution.py:769
  69.0 2.6 %shard_map.121 = (bf16[128,1536]{1,0:T(8,128)(2,1)}, bf16[128,1536]{1,0:T(8,128)(2,1)}, bf16[128,1536]{1,0:T(8,128)(2,1)}, bf16[1,640,768]{2,1,0:T(8,128)(2,1)}) custom-call(bf16[128,1536]{1,0:T(8,128)(2,1)} %get-tuple-element.8.refs_0_, bf16[128,1536]{1,0:T(8,128)(2,1)} %get-tuple-element.9.refs_1_, bf16[128,1536]{1,0:T(8,128)(2,1)} %get-tuple-element.10.refs_2_, ...), custom_call_target="tpu_custom_call" | custom-call | tf_op jit(solution)/shard_map/pallas_call | solution.py:794

commit v5 on v4

--- a/solution.py
+++ b/solution.py
@@ -570,12 +570,13 @@
         for d in range(n_chip):
             zp_copy(z, d).start()
 
+    send_high()
+
     @pl.when(inner == 1)
     def _():
         forward_copy(2).wait_recv()
         forward_copy(2).start()
 
-    send_high()
     per_head(local_parts)
 
     @pl.when(inner == 0)

time: 73 us -> 78.1 us (1.070); the launches traced: 71.6 us -> 77.9 us
  Pallas kernels: 70.9 us -> 77.3 us
    pallas_call x1, Pallas kernels: 68.4 us -> 74.7 us  [fused(): pl.pallas_call(functools.partial(fused_kernel, (n_z, n_chip, cap, heads,...]
where the time goes in v5:
time: 78.1 us; the launch traced here: 77.9 us
  Pallas kernels  77.3 us (99%)
    pallas_call x1, Pallas kernels, fused(): pl.pallas_call(functools.partial(fused_kernel, (n_z, n_chip, cap, heads,...  74.7 us
    pallas_call x1, Pallas kernels, fused(): pl.pallas_call(hand_over, out_shape=tuple((jax.ShapeDtypeStruct(x.shape,...  2.58 us

profile of v5, /device:TPU:0, one launch (start us, length us, event | category | flops | bytes accessed | tf_op | source)
XLA Modules:
  0.0 77.9 jit_solution(3967584874428599047)
XLA Ops:
  0.6 74.7 %shard_map.120 = (bf16[128,1536]{1,0:T(8,128)(2,1)}, bf16[128,1536]{1,0:T(8,128)(2,1)}, bf16[128,1536]{1,0:T(8,128)(2,1)}, bf16[1,640,768]{2,1,0:T(8,128)(2,1)}) custom-call(bf16[128,1536]{1,0:T(8,128)(2,1)} %q_hbm.1, bf16[128,1536]{1,0:T(8,128)(2,1)} %k_hbm.1, bf16[128,1536]{1,0:T(8,128)(2,1)} %v_hbm.1, bf16[128,1536]{1,0:T(8,128)(2,1)} %g_hbm.1, ...), custom_call_target="tpu_custom_call" | custom-call | tf_op jit(solution)/shard_map/pallas_call | solution.py:770
  75.4 2.6 %shard_map.121 = (bf16[128,1536]{1,0:T(8,128)(2,1)}, bf16[128,1536]{1,0:T(8,128)(2,1)}, bf16[128,1536]{1,0:T(8,128)(2,1)}, bf16[1,640,768]{2,1,0:T(8,128)(2,1)}) custom-call(bf16[128,1536]{1,0:T(8,128)(2,1)} %get-tuple-element.8.refs_0_, bf16[128,1536]{1,0:T(8,128)(2,1)} %get-tuple-element.9.refs_1_, bf16[128,1536]{1,0:T(8,128)(2,1)} %get-tuple-element.10.refs_2_, ...), custom_call_target="tpu_custom_call" | custom-call | tf_op jit(solution)/shard_map/pallas_call | solution.py:795
